TPU v7x, 512 devices: a whole 4x8x8 slice. The times are simulated.
512 devices in a mesh: slab: 64 (over z_lo, y, core), lev: 8 (over x, z_hi).
Axes of the slice: x: 4, y: 8, z: 8 (z_hi: 2, z_lo: 4; z = z_hi * 4 + z_lo), core: 2. Of those that a mesh axis runs over, the one named last changes fastest.
Arguments:
- fields: float32 [8, 4, 2048, 2048], P('lev', None, 'slab'), may hold values from -6 to 6
- density: float32 [8], P('lev'), may hold values from 0.3 to 1.2
- inv_thickness: float32 [8], P('lev'), may hold values from 2 to 8
Outputs:
- coarse_fields: float32 [8, 4, 512, 512], P('lev', None, 'slab')
- fluxes: float32 [8, 4, 512, 512], P('lev', None, 'slab')
- tendency: float32 [8, 3, 512, 512], P('lev', None, 'slab')
All inputs are finite; a program needn't handle non-finite values.
Results may differ from a plain program's by a relative error of at most 0.0003.
Values sent between devices are 32-bit elements; how exact they have to be, the bound alone decides.
A program may use at most 64 MiB of HBM per device.

v0:
```python
import functools

import jax
import jax.numpy as jnp
import ml_dtypes
import numpy as np
from jax import lax
from jax.experimental import pallas as pl
from jax.experimental.pallas import tpu as pltpu
from jax.sharding import PartitionSpec as P

GRID = 2048
TARGET = 512
ORDER = (2, 1, 3, 0)
F32 = jnp.float32
BF16 = jnp.bfloat16


def tables():
    k = np.arange(1, TARGET // 2, dtype=np.float64)
    offsets = np.arange(GRID, dtype=np.float64)
    profile = (1.0 + 2.0 * np.cos(2.0 * np.pi * np.outer(offsets, k) / GRID).sum(1)) / GRID
    index = (GRID // TARGET * np.arange(TARGET)[:, None] - np.arange(GRID)[None, :]) % GRID
    matrix = profile[index].astype(np.float32)
    columns = np.ascontiguousarray(matrix[:128].T)
    first = matrix[:, :512].reshape(4, 8, 2, 8, 8, 2, 32)
    rows = [
        np.stack([first[:, :, c, :, :, core] for c in (1 - core, core)], axis=1).reshape(4, 128, 256)
        for core in range(2)
    ]
    return columns, np.stack(rows)


def split(value):
    high = value.astype(BF16)
    return high, (value - high.astype(F32)).astype(BF16)


def dot(a, b):
    return jnp.dot(a, b, preferred_element_type=F32)


def kernel(
    fields, density, thickness, col_hbm, row_hbm, coarse_out, flux_out, tend_out,
    g_in, col_in, row_in, col, row, g_high, g_low, send, recv, acc, part_in, osend, orecv, wsend, wrecv,
    load_sem, send_sem, recv_sem, part_sem, osend_sem, orecv_sem, wsend_sem, wrecv_sem,
):
    slab, lev = lax.axis_index("slab"), lax.axis_index("lev")
    core, chip = lax.rem(slab, 2), lax.div(slab, 2)
    z, y = lax.div(chip, 8), lax.rem(chip, 8)
    has_up, has_down = lev < 7, lev > 0

    load = pltpu.make_async_copy(fields.at[0], g_in, load_sem.at[0])
    load.start()
    col_load = pltpu.make_async_copy(col_hbm, col_in, load_sem.at[1])
    col_load.start()
    row_load = pltpu.make_async_copy(row_hbm.at[core], row_in, load_sem.at[2])
    row_load.start()

    barrier = pltpu.get_barrier_semaphore()

    def greet(s, carry):
        peer = lax.rem(chip + s, 32)
        pl.semaphore_signal(barrier, inc=1, device_id={"slab": 2 * peer + core})
        return carry

    lax.fori_loop(1, 32, greet, 0)
    pl.semaphore_signal(barrier, inc=1, device_id={"slab": 2 * chip + 1 - core})

    @pl.when(has_up)
    def _():
        pl.semaphore_signal(barrier, inc=1, device_id={"lev": lev + 1})

    @pl.when(has_down)
    def _():
        pl.semaphore_signal(barrier, inc=1, device_id={"lev": lev - 1})

    load.wait()
    for f in range(4):
        h, l = split(g_in[f])
        g_high[32 * f : 32 * f + 32] = h
        g_low[32 * f : 32 * f + 32] = l
    for f, (a, b) in enumerate(((0, 2), (1, 2), (3, 2), (0, 1))):
        h, l = split(g_in[a] * g_in[b])
        g_high[128 + 32 * f : 160 + 32 * f] = h
        g_low[128 + 32 * f : 160 + 32 * f] = l

    col_load.wait()
    h, l = split(col_in[...])
    col[:GRID, :128], col[:GRID, 128:] = h, l
    col[GRID:, :128], col[GRID:, 128:] = h[:1536], l[:1536]

    for n, k in enumerate(ORDER):
        zq = lax.rem(z + k, 4)
        turn = pl.ds(pl.multiple_of(512 * lax.rem(4 - zq, 4), 512), GRID)
        both = dot(g_high[...], col[turn])
        extra = dot(g_low[...], col[turn, :128])
        send[n] = both[:, :128] + both[:, 128:] + extra
        if n == 0:
            pl.semaphore_wait(barrier, 32 + has_up.astype(jnp.int32) + has_down.astype(jnp.int32))

        def push(s, carry, n=n, zq=zq):
            yq = lax.rem(y + s, 8)
            pltpu.make_async_remote_copy(
                src_ref=send.at[n, pl.ds(yq * 32, 32)],
                dst_ref=recv.at[z, pl.ds(y * 32, 32)],
                send_sem=send_sem.at[n],
                recv_sem=recv_sem.at[z],
                device_id={"slab": (zq * 8 + yq) * 2 + core},
            ).start()
            return carry

        lax.fori_loop(0 if k else 1, 8, push, 0)
        if k == 0:
            recv[z, pl.ds(y * 32, 32)] = send[n, pl.ds(y * 32, 32)]

    row_load.wait()
    h, l = split(row_in[...])
    row[0, :4], row[1, :4] = h, l
    row[0, 4:], row[1, 4:] = h[:3], l[:3]

    for n, k in enumerate(ORDER):
        zs = lax.rem(z + 4 - k, 4)
        size = 256 if k else 224
        pltpu.make_async_copy(recv.at[zs, pl.ds(0, size)], recv.at[zs, pl.ds(0, size)], recv_sem.at[zs]).wait()
        h, l = split(recv[zs])
        turn = pl.ds(lax.rem(4 - zs, 4), 4)
        both = dot(row[0, turn].reshape(512, 256), jnp.concatenate([h, l], axis=1))
        extra = dot(row[1, turn].reshape(512, 256), h)
        total = (both[:, :128] + both[:, 128:] + extra).reshape(4, 128, 128)
        if n:
            acc[...] += total
        else:
            acc[...] = total

    def cross(n):
        zq = lax.rem(z + ORDER[n], 4)
        return pltpu.make_async_remote_copy(
            src_ref=acc.at[zq, pl.ds(0, 64)],
            dst_ref=part_in.at[n],
            send_sem=part_sem.at[0, n],
            recv_sem=part_sem.at[1, n],
            device_id={"slab": 2 * chip + 1 - core},
        )

    for n in range(4):
        cross(n).start()

    for n, k in enumerate(ORDER):
        zq = lax.rem(z + k, 4)
        cross(n).wait_recv()
        osend[n] = acc[zq, 64:] + part_in[n]

        def give(s, carry, n=n, zq=zq):
            yq = lax.rem(y + s, 8)
            pltpu.make_async_remote_copy(
                src_ref=osend.at[n, pl.ds(yq * 8, 8)],
                dst_ref=orecv.at[z, pl.ds(y * 8, 8)],
                send_sem=osend_sem.at[n],
                recv_sem=orecv_sem.at[z],
                device_id={"slab": (zq * 8 + yq) * 2 + core},
            ).start()
            return carry

        lax.fori_loop(0 if k else 1, 8, give, 0)
        if k == 0:
            orecv[z, pl.ds(y * 8, 8)] = osend[n, pl.ds(y * 8, 8)]

    def lev_copy(n, side):
        return pltpu.make_async_remote_copy(
            src_ref=wsend.at[n],
            dst_ref=wrecv.at[side, n],
            send_sem=wsend_sem.at[side, n],
            recv_sem=wrecv_sem.at[side, n],
            device_id={"lev": lev + 1 if side == 0 else lev - 1},
        )

    for n, k in enumerate(ORDER):
        zs = lax.rem(z + 4 - k, 4)
        size = 64 if k else 56
        pltpu.make_async_copy(orecv.at[zs, pl.ds(0, size)], orecv.at[zs, pl.ds(0, size)], orecv_sem.at[zs]).wait()
        tile = [orecv[zs, 8 * f : 8 * f + 8] for f in range(8)]
        lanes = pl.ds(pl.multiple_of(zs * 128, 128), 128)
        for f in range(4):
            coarse_out[0, f, :, lanes] = tile[f]
        for f, (a, b) in enumerate(((0, 2), (1, 2), (3, 2), (0, 1))):
            flux = tile[4 + f] - tile[a] * tile[b]
            flux_out[0, f, :, lanes] = flux
            if f < 3:
                wsend[n, 8 * f : 8 * f + 8] = density[0] * flux

        @pl.when(has_up)
        def _(n=n):
            lev_copy(n, 0).start()

        @pl.when(has_down)
        def _(n=n):
            lev_copy(n, 1).start()

    @pl.when(jnp.logical_not(has_down))
    def _():
        wrecv[0] = jnp.zeros_like(wrecv[0])

    @pl.when(jnp.logical_not(has_up))
    def _():
        wrecv[1] = jnp.zeros_like(wrecv[1])

    factor = thickness[0] / (2.0 * density[0])
    for n, k in enumerate(ORDER):
        zs = lax.rem(z + 4 - k, 4)
        lanes = pl.ds(pl.multiple_of(zs * 128, 128), 128)

        @pl.when(has_down)
        def _(n=n):
            lev_copy(n, 0).wait_recv()

        @pl.when(has_up)
        def _(n=n):
            lev_copy(n, 1).wait_recv()

        for f in range(3):
            rows = slice(8 * f, 8 * f + 8)
            tend_out[0, f, :, lanes] = -(wrecv[1, n, rows] - wrecv[0, n, rows]) * factor

    for n, k in enumerate(ORDER):
        size = 256 if k else 224
        pltpu.make_async_copy(send.at[n, pl.ds(0, size)], send.at[n, pl.ds(0, size)], send_sem.at[n]).wait()
        size = 64 if k else 56
        pltpu.make_async_copy(osend.at[n, pl.ds(0, size)], osend.at[n, pl.ds(0, size)], osend_sem.at[n]).wait()
        cross(n).wait_send()

        @pl.when(has_up)
        def _(n=n):
            lev_copy(n, 0).wait_send()

        @pl.when(has_down)
        def _(n=n):
            lev_copy(n, 1).wait_send()


def shards(columns, rows, fields, density, thickness):
    anywhere = pl.BlockSpec(memory_space=pl.ANY)
    scalar = pl.BlockSpec(memory_space=pltpu.SMEM)
    vmem = pl.BlockSpec(memory_space=pltpu.VMEM)
    dma = pltpu.SemaphoreType.DMA
    return pl.pallas_call(
        kernel,
        out_shape=[jax.ShapeDtypeStruct((1, n, 8, TARGET), F32) for n in (4, 4, 3)],
        in_specs=[anywhere, scalar, scalar, anywhere, anywhere],
        out_specs=[vmem] * 3,
        scratch_shapes=[
            pltpu.VMEM((4, 32, GRID), F32),
            pltpu.VMEM((GRID, 128), F32),
            pltpu.VMEM((4, 128, 256), F32),
            pltpu.VMEM((GRID + 1536, 256), BF16),
            pltpu.VMEM((2, 7, 128, 256), BF16),
            pltpu.VMEM((256, GRID), BF16),
            pltpu.VMEM((256, GRID), BF16),
            pltpu.VMEM((4, 256, 128), F32),
            pltpu.VMEM((4, 256, 128), F32),
            pltpu.VMEM((4, 128, 128), F32),
            pltpu.VMEM((4, 64, 128), F32),
            pltpu.VMEM((4, 64, 128), F32),
            pltpu.VMEM((4, 64, 128), F32),
            pltpu.VMEM((4, 24, 128), F32),
            pltpu.VMEM((2, 4, 24, 128), F32),
            dma((3,)),
            dma((4,)),
            dma((4,)),
            dma((2, 4)),
            dma((4,)),
            dma((4,)),
            dma((2, 4)),
            dma((2, 4)),
        ],
        compiler_params=pltpu.CompilerParams(
            collective_id=0, has_side_effects=True, vmem_limit_bytes=40 * 1024 * 1024
        ),
    )(fields, density, thickness, columns, rows)


def solution(mesh):
    columns, rows = tables()
    placed = P("lev", None, "slab", None)
    return jax.shard_map(
        functools.partial(shards, columns, rows),
        mesh=mesh,
        in_specs=(placed, P("lev"), P("lev")),
        out_specs=(placed, placed, placed),
        check_vma=False,
    )
```

profile of v0, /device:TPU:1, one launch (start us, length us, event | category | flops | bytes accessed | tf_op | source)
XLA Modules:
  0.0 52.0 jit_solution(12706337429838828075)
XLA Ops:
  1.9 0.0 copy-start
  1.9 1.2 %copy-done = f32[1,4,32,2048]{3,2,1,0:T(8,128)S(1)} copy-done((f32[1,4,32,2048]{3,2,1,0:T(8,128)S(1)}, f32[1,4,32,2048]{3,2,1,0:T(8,128)}, u32[]{:S(2)}) %copy-start) | copy-done | bytes 1048600
  3.1 0.0 copy-start.1
  3.1 1.2 %copy-done.1 = f32[2,4,128,256]{3,2,1,0:T(8,128)S(1)} copy-done((f32[2,4,128,256]{3,2,1,0:T(8,128)S(1)}, f32[2,4,128,256]{3,2,1,0:T(8,128)}, u32[]{:S(2)}) %copy-start.1) | copy-done | bytes 1048600
  4.4 0.0 copy-start.2
  4.4 1.2 %copy-done.2 = f32[2048,128]{1,0:T(8,128)S(1)} copy-done((f32[2048,128]{1,0:T(8,128)S(1)}, f32[2048,128]{1,0:T(8,128)}, u32[]{:S(2)}) %copy-start.2) | copy-done | bytes 1048600
  5.6 44.5 %shard_map.76 = (f32[1,4,8,512]{3,2,1,0:T(8,128)S(1)}, f32[1,4,8,512]{3,2,1,0:T(8,128)S(1)}, f32[1,3,8,512]{3,2,1,0:T(8,128)S(1)}) custom-call(f32[1,4,32,2048]{3,2,1,0:T(8,128)S(1)} %copy-done, f32[1]{0:T(128)S(6)} %copy.11.density, f32[1]{0:T(128)S(6)} %copy.12.thickness, f32[2048,128]{1,0:T(8,128)S(1)} %copy-done.2, f32[2,4,128,256]{3,2,1,0:T(8,128)S(1)} %copy-done.1), custom_call_target="tpu_custom_call" | custom-call | tf_op jit(solution)/shard_map/pallas_call | solution.py:246
  50.1 0.6 %copy.13 = f32[1,4,8,512]{3,2,1,0:T(8,128)} copy(f32[1,4,8,512]{3,2,1,0:T(8,128)S(1)} %get-tuple-element.6) | data formatting | bytes 131072
  50.8 0.6 %copy.14 = f32[1,4,8,512]{3,2,1,0:T(8,128)} copy(f32[1,4,8,512]{3,2,1,0:T(8,128)S(1)} %get-tuple-element.7) | data formatting | bytes 131072
  51.4 0.6 %copy.15 = f32[1,3,8,512]{3,2,1,0:T(8,128)} copy(f32[1,3,8,512]{3,2,1,0:T(8,128)S(1)} %get-tuple-element.8) | data formatting | bytes 98304
Async XLA Ops:
  1.9 1.2 %copy-start = (f32[1,4,32,2048]{3,2,1,0:T(8,128)S(1)}, f32[1,4,32,2048]{3,2,1,0:T(8,128)}, u32[]{:S(2)}) copy-start(f32[1,4,32,2048]{3,2,1,0:T(8,128)} %fields.1) | copy-start | bytes 3145732
  3.1 1.2 %copy-start.1 = (f32[2,4,128,256]{3,2,1,0:T(8,128)S(1)}, f32[2,4,128,256]{3,2,1,0:T(8,128)}, u32[]{:S(2)}) copy-start(f32[2,4,128,256]{3,2,1,0:T(8,128)} %constant.5.clone.row_hbm) | copy-start | bytes 3145732
  4.4 1.2 %copy-start.2 = (f32[2048,128]{1,0:T(8,128)S(1)}, f32[2048,128]{1,0:T(8,128)}, u32[]{:S(2)}) copy-start(f32[2048,128]{1,0:T(8,128)} %constant.4.clone.col_hbm) | copy-start | bytes 3145732
where the time goes:
time: 53 us; the launch traced here: 52 us
  Pallas kernels  44.5 us (84%)
  local copies, waits for them, and re-layouts  5.55 us (10%)
  between operations  1.94 us (4%)
    pallas_call x1, Pallas kernels, shards(): pl.pallas_call(kernel, out_shape=[jax.ShapeDtypeStruct((1, n, 8, TARGET),...  44.5 us
    unnamed x9, local copies, waits for them, and re-layouts  5.55 us

commit v1 on v0

--- a/solution.py
+++ b/solution.py
@@ -12,6 +12,8 @@
 GRID = 2048
 TARGET = 512
 ORDER = (2, 1, 3, 0)
+AROUND = (0, 4, 1, 5, 2, 6, 3, 7)
+NEAREST = ((0, 1, 2, 3), (1, 0, 2, 3), (2, 3, 1, 0), (3, 2, 1, 0))
 F32 = jnp.float32
 BF16 = jnp.bfloat16
 
@@ -41,14 +43,15 @@
 
 
 def kernel(
-    fields, density, thickness, col_hbm, row_hbm, coarse_out, flux_out, tend_out,
-    g_in, col_in, row_in, col, row, g_high, g_low, send, recv, acc, part_in, osend, orecv, wsend, wrecv,
+    fields, density_hbm, thickness_hbm, col_hbm, row_hbm, out,
+    density, thickness, g_in, col_in, row_in, col, row, g_high, g_low, send, recv, acc, part_in, osend, orecv, wsend, wrecv,
     load_sem, send_sem, recv_sem, part_sem, osend_sem, orecv_sem, wsend_sem, wrecv_sem,
 ):
     slab, lev = lax.axis_index("slab"), lax.axis_index("lev")
     core, chip = lax.rem(slab, 2), lax.div(slab, 2)
     z, y = lax.div(chip, 8), lax.rem(chip, 8)
     has_up, has_down = lev < 7, lev > 0
+    near = [jnp.where(z < 2, jnp.where(z == 0, a, b), jnp.where(z == 2, c, d)) for a, b, c, d in zip(*NEAREST)]
 
     load = pltpu.make_async_copy(fields.at[0], g_in, load_sem.at[0])
     load.start()
@@ -56,6 +59,12 @@
     col_load.start()
     row_load = pltpu.make_async_copy(row_hbm.at[core], row_in, load_sem.at[2])
     row_load.start()
+    scalars = [
+        pltpu.make_async_copy(density_hbm, density, load_sem.at[3]),
+        pltpu.make_async_copy(thickness_hbm, thickness, load_sem.at[4]),
+    ]
+    for c in scalars:
+        c.start()
 
     barrier = pltpu.get_barrier_semaphore()
 
@@ -99,8 +108,8 @@
         if n == 0:
             pl.semaphore_wait(barrier, 32 + has_up.astype(jnp.int32) + has_down.astype(jnp.int32))
 
-        def push(s, carry, n=n, zq=zq):
-            yq = lax.rem(y + s, 8)
+        for step in AROUND[0 if k else 1 :]:
+            yq = lax.rem(y + step, 8)
             pltpu.make_async_remote_copy(
                 src_ref=send.at[n, pl.ds(yq * 32, 32)],
                 dst_ref=recv.at[z, pl.ds(y * 32, 32)],
@@ -108,16 +117,24 @@
                 recv_sem=recv_sem.at[z],
                 device_id={"slab": (zq * 8 + yq) * 2 + core},
             ).start()
-            return carry
-
-        lax.fori_loop(0 if k else 1, 8, push, 0)
         if k == 0:
             recv[z, pl.ds(y * 32, 32)] = send[n, pl.ds(y * 32, 32)]
 
     row_load.wait()
+    for c in scalars:
+        c.wait()
     h, l = split(row_in[...])
     row[0, :4], row[1, :4] = h, l
     row[0, 4:], row[1, 4:] = h[:3], l[:3]
+
+    def cross(i):
+        return pltpu.make_async_remote_copy(
+            src_ref=acc.at[0, near[i]],
+            dst_ref=part_in.at[i],
+            send_sem=part_sem.at[0, i],
+            recv_sem=part_sem.at[1, i],
+            device_id={"slab": 2 * chip + 1 - core},
+        )
 
     for n, k in enumerate(ORDER):
         zs = lax.rem(z + 4 - k, 4)
@@ -125,46 +142,35 @@
         pltpu.make_async_copy(recv.at[zs, pl.ds(0, size)], recv.at[zs, pl.ds(0, size)], recv_sem.at[zs]).wait()
         h, l = split(recv[zs])
         turn = pl.ds(lax.rem(4 - zs, 4), 4)
-        both = dot(row[0, turn].reshape(512, 256), jnp.concatenate([h, l], axis=1))
-        extra = dot(row[1, turn].reshape(512, 256), h)
-        total = (both[:, :128] + both[:, 128:] + extra).reshape(4, 128, 128)
-        if n:
-            acc[...] += total
-        else:
-            acc[...] = total
-
-    def cross(n):
-        zq = lax.rem(z + ORDER[n], 4)
-        return pltpu.make_async_remote_copy(
-            src_ref=acc.at[zq, pl.ds(0, 64)],
-            dst_ref=part_in.at[n],
-            send_sem=part_sem.at[0, n],
-            recv_sem=part_sem.at[1, n],
-            device_id={"slab": 2 * chip + 1 - core},
-        )
-
-    for n in range(4):
-        cross(n).start()
-
-    for n, k in enumerate(ORDER):
-        zq = lax.rem(z + k, 4)
-        cross(n).wait_recv()
-        osend[n] = acc[zq, 64:] + part_in[n]
-
-        def give(s, carry, n=n, zq=zq):
-            yq = lax.rem(y + s, 8)
+        pair = jnp.concatenate([h, l], axis=1)
+        for half in range(2):
+            part = slice(64 * half, 64 * half + 64)
+            both = dot(row[0, turn, part].reshape(256, 256), pair)
+            extra = dot(row[1, turn, part].reshape(256, 256), h)
+            total = (both[:, :128] + both[:, 128:] + extra).reshape(4, 64, 128)
+            if n:
+                acc[half] += total
+            else:
+                acc[half] = total
+            if n == 3 and half == 0:
+                for i in reversed(range(4)):
+                    cross(i).start()
+
+    for i in reversed(range(4)):
+        zq = near[i]
+        cross(i).wait_recv()
+        osend[i] = acc[1, zq] + part_in[i]
+        for step in AROUND[0 if i else 1 :]:
+            yq = lax.rem(y + step, 8)
             pltpu.make_async_remote_copy(
-                src_ref=osend.at[n, pl.ds(yq * 8, 8)],
+                src_ref=osend.at[i, pl.ds(yq * 8, 8)],
                 dst_ref=orecv.at[z, pl.ds(y * 8, 8)],
-                send_sem=osend_sem.at[n],
+                send_sem=osend_sem.at[i],
                 recv_sem=orecv_sem.at[z],
                 device_id={"slab": (zq * 8 + yq) * 2 + core},
             ).start()
-            return carry
-
-        lax.fori_loop(0 if k else 1, 8, give, 0)
-        if k == 0:
-            orecv[z, pl.ds(y * 8, 8)] = osend[n, pl.ds(y * 8, 8)]
+        if i == 0:
+            orecv[z, pl.ds(y * 8, 8)] = osend[i, pl.ds(y * 8, 8)]
 
     def lev_copy(n, side):
         return pltpu.make_async_remote_copy(
@@ -175,17 +181,17 @@
             device_id={"lev": lev + 1 if side == 0 else lev - 1},
         )
 
-    for n, k in enumerate(ORDER):
-        zs = lax.rem(z + 4 - k, 4)
-        size = 64 if k else 56
+    for n in range(4):
+        zs = near[n]
+        size = 64 if n else 56
         pltpu.make_async_copy(orecv.at[zs, pl.ds(0, size)], orecv.at[zs, pl.ds(0, size)], orecv_sem.at[zs]).wait()
         tile = [orecv[zs, 8 * f : 8 * f + 8] for f in range(8)]
         lanes = pl.ds(pl.multiple_of(zs * 128, 128), 128)
         for f in range(4):
-            coarse_out[0, f, :, lanes] = tile[f]
+            out[f, :, lanes] = tile[f]
         for f, (a, b) in enumerate(((0, 2), (1, 2), (3, 2), (0, 1))):
             flux = tile[4 + f] - tile[a] * tile[b]
-            flux_out[0, f, :, lanes] = flux
+            out[4 + f, :, lanes] = flux
             if f < 3:
                 wsend[n, 8 * f : 8 * f + 8] = density[0] * flux
 
@@ -206,8 +212,8 @@
         wrecv[1] = jnp.zeros_like(wrecv[1])
 
     factor = thickness[0] / (2.0 * density[0])
-    for n, k in enumerate(ORDER):
-        zs = lax.rem(z + 4 - k, 4)
+    for n in range(4):
+        zs = near[n]
         lanes = pl.ds(pl.multiple_of(zs * 128, 128), 128)
 
         @pl.when(has_down)
@@ -220,12 +226,12 @@
 
         for f in range(3):
             rows = slice(8 * f, 8 * f + 8)
-            tend_out[0, f, :, lanes] = -(wrecv[1, n, rows] - wrecv[0, n, rows]) * factor
+            out[8 + f, :, lanes] = -(wrecv[1, n, rows] - wrecv[0, n, rows]) * factor
 
     for n, k in enumerate(ORDER):
         size = 256 if k else 224
         pltpu.make_async_copy(send.at[n, pl.ds(0, size)], send.at[n, pl.ds(0, size)], send_sem.at[n]).wait()
-        size = 64 if k else 56
+        size = 64 if n else 56
         pltpu.make_async_copy(osend.at[n, pl.ds(0, size)], osend.at[n, pl.ds(0, size)], osend_sem.at[n]).wait()
         cross(n).wait_send()
 
@@ -239,16 +245,17 @@
 
 
 def shards(columns, rows, fields, density, thickness):
-    anywhere = pl.BlockSpec(memory_space=pl.ANY)
-    scalar = pl.BlockSpec(memory_space=pltpu.SMEM)
+    hbm = pl.BlockSpec(memory_space=pltpu.HBM)
     vmem = pl.BlockSpec(memory_space=pltpu.VMEM)
     dma = pltpu.SemaphoreType.DMA
-    return pl.pallas_call(
+    out = pl.pallas_call(
         kernel,
-        out_shape=[jax.ShapeDtypeStruct((1, n, 8, TARGET), F32) for n in (4, 4, 3)],
-        in_specs=[anywhere, scalar, scalar, anywhere, anywhere],
-        out_specs=[vmem] * 3,
+        out_shape=jax.ShapeDtypeStruct((11, 8, TARGET), F32),
+        in_specs=[hbm] * 5,
+        out_specs=vmem,
         scratch_shapes=[
+            pltpu.SMEM((1,), F32),
+            pltpu.SMEM((1,), F32),
             pltpu.VMEM((4, 32, GRID), F32),
             pltpu.VMEM((GRID, 128), F32),
             pltpu.VMEM((4, 128, 256), F32),
@@ -258,13 +265,13 @@
             pltpu.VMEM((256, GRID), BF16),
             pltpu.VMEM((4, 256, 128), F32),
             pltpu.VMEM((4, 256, 128), F32),
-            pltpu.VMEM((4, 128, 128), F32),
+            pltpu.VMEM((2, 4, 64, 128), F32),
             pltpu.VMEM((4, 64, 128), F32),
             pltpu.VMEM((4, 64, 128), F32),
             pltpu.VMEM((4, 64, 128), F32),
             pltpu.VMEM((4, 24, 128), F32),
             pltpu.VMEM((2, 4, 24, 128), F32),
-            dma((3,)),
+            dma((5,)),
             dma((4,)),
             dma((4,)),
             dma((2, 4)),
@@ -274,9 +281,10 @@
             dma((2, 4)),
         ],
         compiler_params=pltpu.CompilerParams(
-            collective_id=0, has_side_effects=True, vmem_limit_bytes=40 * 1024 * 1024
+            collective_id=0, has_side_effects=True, vmem_limit_bytes=54528 * 1024
         ),
     )(fields, density, thickness, columns, rows)
+    return out[None, :4], out[None, 4:8], out[None, 8:]
 
 
 def solution(mesh):

time: 53 us -> 47.7 us (0.900); the launches traced: 52 us -> 47.5 us
  local copies, waits for them, and re-layouts: 5.55 us -> 1.28 us
    unnamed x9 -> x0, local copies, waits for them, and re-layouts: 5.55 us -> none
    broadcast_in_dim x0 -> x2, local copies, waits for them, and re-layouts: none -> 1.28 us  [shards(): return (out[None, :4], out[None, 4:8], out[None, 8:])]
where the time goes in v1:
time: 47.7 us; the launch traced here: 47.5 us
  Pallas kernels  44.2 us (93%)
  between operations  1.93 us (4%)
  local copies, waits for them, and re-layouts  1.28 us (3%)
    pallas_call x1, Pallas kernels, shards(): pl.pallas_call(kernel, out_shape=jax.ShapeDtypeStruct((11, 8, TARGET), F3...  44.2 us
    broadcast_in_dim x2, local copies, waits for them, and re-layouts, shards(): return (out[None, :4], out[None, 4:8], out[None, 8:])  1.28 us

profile of v1, /device:TPU:1, one launch (start us, length us, event | category | flops | bytes accessed | tf_op | source)
XLA Modules:
  0.0 47.5 jit_solution(17471324091991252934)
XLA Ops:
  1.9 44.2 %shard_map.76 = f32[11,8,512]{2,1,0:T(8,128)S(1)} custom-call(f32[1,4,32,2048]{3,2,1,0:T(8,128)} %fields.1, f32[1]{0:T(128)S(6)} %copy.8.density_hbm, f32[1]{0:T(128)S(6)} %copy.9.thickness_hbm, f32[2048,128]{1,0:T(8,128)} %constant.4.clone.col_hbm, f32[2,4,128,256]{3,2,1,0:T(8,128)} %constant.5.clone.row_hbm), custom_call_target="tpu_custom_call" | custom-call | tf_op jit(solution)/shard_map/pallas_call | solution.py:251
  46.2 0.7 %slice_bitcast_fusion = (f32[1,4,8,512]{3,2,1,0:T(8,128)}, f32[1,4,8,512]{3,2,1,0:T(8,128)}) fusion(f32[11,8,512]{2,1,0:T(8,128)S(1)} %shard_map.76), kind=kLoop, calls=%fused_computation | loop fusion | bytes 262144 | tf_op jit(solution)/shard_map/broadcast_in_dim | solution.py:287
  46.8 0.6 %slice_bitcast_fusion.2 = f32[1,3,8,512]{3,2,1,0:T(8,128)} fusion(f32[11,8,512]{2,1,0:T(8,128)S(1)} %shard_map.76), kind=kLoop, calls=%fused_computation.2 | loop fusion | bytes 98304 | tf_op jit(solution)/shard_map/broadcast_in_dim | solution.py:287

commit v2 on v1

--- a/solution.py
+++ b/solution.py
@@ -11,7 +11,9 @@
 
 GRID = 2048
 TARGET = 512
+SENT = 25
 ORDER = (2, 1, 3, 0)
+PRODUCTS = ((0, 2), (1, 2), (3, 2), (0, 1))
 AROUND = (0, 4, 1, 5, 2, 6, 3, 7)
 NEAREST = ((0, 1, 2, 3), (1, 0, 2, 3), (2, 3, 1, 0), (3, 2, 1, 0))
 F32 = jnp.float32
@@ -25,9 +27,9 @@
     index = (GRID // TARGET * np.arange(TARGET)[:, None] - np.arange(GRID)[None, :]) % GRID
     matrix = profile[index].astype(np.float32)
     columns = np.ascontiguousarray(matrix[:128].T)
-    first = matrix[:, :512].reshape(4, 8, 2, 8, 8, 2, 32)
+    first = matrix[:, :512].reshape(4, 8, 2, 8, 8, 2, 8, 4)[..., 1:].swapaxes(6, 7)
     rows = [
-        np.stack([first[:, :, c, :, :, core] for c in (1 - core, core)], axis=1).reshape(4, 128, 256)
+        np.stack([first[:, :, c, :, :, core] for c in (1 - core, core)], axis=1).reshape(4, 128, 192)
         for core in range(2)
     ]
     return columns, np.stack(rows)
@@ -44,7 +46,7 @@
 
 def kernel(
     fields, density_hbm, thickness_hbm, col_hbm, row_hbm, out,
-    density, thickness, g_in, col_in, row_in, col, row, g_high, g_low, send, recv, acc, part_in, osend, orecv, wsend, wrecv,
+    density, thickness, g_in, col_in, row_in, col, row, g_high, g_low, whole, send, recv, local, acc, part_in, osend, orecv, wsend, wrecv,
     load_sem, send_sem, recv_sem, part_sem, osend_sem, orecv_sem, wsend_sem, wrecv_sem,
 ):
     slab, lev = lax.axis_index("slab"), lax.axis_index("lev")
@@ -68,12 +70,10 @@
 
     barrier = pltpu.get_barrier_semaphore()
 
-    def greet(s, carry):
-        peer = lax.rem(chip + s, 32)
-        pl.semaphore_signal(barrier, inc=1, device_id={"slab": 2 * peer + core})
-        return carry
-
-    lax.fori_loop(1, 32, greet, 0)
+    for i in reversed(range(4)):
+        for step in AROUND[0 if i else 1 :]:
+            peer = near[i] * 8 + lax.rem(y + step, 8)
+            pl.semaphore_signal(barrier, inc=1, device_id={"slab": 2 * peer + core})
     pl.semaphore_signal(barrier, inc=1, device_id={"slab": 2 * chip + 1 - core})
 
     @pl.when(has_up)
@@ -85,40 +85,45 @@
         pl.semaphore_signal(barrier, inc=1, device_id={"lev": lev - 1})
 
     load.wait()
-    for f in range(4):
-        h, l = split(g_in[f])
+    fine = [g_in[f] for f in range(4)]
+    fine += [fine[a] * fine[b] for a, b in PRODUCTS]
+    for f in range(8):
+        h, l = split(fine[f])
         g_high[32 * f : 32 * f + 32] = h
         g_low[32 * f : 32 * f + 32] = l
-    for f, (a, b) in enumerate(((0, 2), (1, 2), (3, 2), (0, 1))):
-        h, l = split(g_in[a] * g_in[b])
-        g_high[128 + 32 * f : 160 + 32 * f] = h
-        g_low[128 + 32 * f : 160 + 32 * f] = l
 
     col_load.wait()
     h, l = split(col_in[...])
     col[:GRID, :128], col[:GRID, 128:] = h, l
     col[GRID:, :128], col[GRID:, 128:] = h[:1536], l[:1536]
 
+    alternating = 1.0 - 2.0 * lax.rem(lax.broadcasted_iota(jnp.int32, (8, 128), 0), 2).astype(F32)
     for n, k in enumerate(ORDER):
         zq = lax.rem(z + k, 4)
         turn = pl.ds(pl.multiple_of(512 * lax.rem(4 - zq, 4), 512), GRID)
         both = dot(g_high[...], col[turn])
         extra = dot(g_low[...], col[turn, :128])
-        send[n] = both[:, :128] + both[:, 128:] + extra
+        whole[...] = both[:, :128] + both[:, 128:] + extra
+        for f in range(8):
+            for s in (1, 2, 3):
+                send[n, f, 8 * s - 8 : 8 * s] = whole[pl.ds(32 * f + s, 8, 4)]
+            kept = whole[pl.ds(32 * f, 8, 4)]
+            send[n, f, 24:25] = jnp.sum(kept * alternating, axis=0, keepdims=True)
+            local[zq, f] = 0.25 * kept
         if n == 0:
             pl.semaphore_wait(barrier, 32 + has_up.astype(jnp.int32) + has_down.astype(jnp.int32))
 
         for step in AROUND[0 if k else 1 :]:
             yq = lax.rem(y + step, 8)
             pltpu.make_async_remote_copy(
-                src_ref=send.at[n, pl.ds(yq * 32, 32)],
-                dst_ref=recv.at[z, pl.ds(y * 32, 32)],
+                src_ref=send.at[n, yq, pl.ds(0, SENT)],
+                dst_ref=recv.at[z, y, pl.ds(0, SENT)],
                 send_sem=send_sem.at[n],
                 recv_sem=recv_sem.at[z],
                 device_id={"slab": (zq * 8 + yq) * 2 + core},
             ).start()
         if k == 0:
-            recv[z, pl.ds(y * 32, 32)] = send[n, pl.ds(y * 32, 32)]
+            recv[z, y] = send[n, y]
 
     row_load.wait()
     for c in scalars:
@@ -138,16 +143,18 @@
 
     for n, k in enumerate(ORDER):
         zs = lax.rem(z + 4 - k, 4)
-        size = 256 if k else 224
-        pltpu.make_async_copy(recv.at[zs, pl.ds(0, size)], recv.at[zs, pl.ds(0, size)], recv_sem.at[zs]).wait()
-        h, l = split(recv[zs])
+        arrived = recv.at[zs, pl.ds(0, 8 if k else 7), pl.ds(0, SENT)]
+        pltpu.make_async_copy(arrived, arrived, recv_sem.at[zs]).wait()
+        h, l = split(recv[zs, :, :24].reshape(192, 128))
+        removed = jnp.sum(recv[zs, :, 24], axis=0, keepdims=True) * alternating * (1.0 / GRID)
         turn = pl.ds(lax.rem(4 - zs, 4), 4)
         pair = jnp.concatenate([h, l], axis=1)
         for half in range(2):
             part = slice(64 * half, 64 * half + 64)
-            both = dot(row[0, turn, part].reshape(256, 256), pair)
-            extra = dot(row[1, turn, part].reshape(256, 256), h)
-            total = (both[:, :128] + both[:, 128:] + extra).reshape(4, 64, 128)
+            both = dot(row[0, turn, part].reshape(256, 192), pair)
+            extra = dot(row[1, turn, part].reshape(256, 192), h)
+            total = (both[:, :128] + both[:, 128:] + extra).reshape(4, 8, 8, 128)
+            total = (total - removed).reshape(4, 64, 128)
             if n:
                 acc[half] += total
             else:
@@ -185,11 +192,11 @@
         zs = near[n]
         size = 64 if n else 56
         pltpu.make_async_copy(orecv.at[zs, pl.ds(0, size)], orecv.at[zs, pl.ds(0, size)], orecv_sem.at[zs]).wait()
-        tile = [orecv[zs, 8 * f : 8 * f + 8] for f in range(8)]
+        tile = [orecv[zs, 8 * f : 8 * f + 8] + local[zs, f] for f in range(8)]
         lanes = pl.ds(pl.multiple_of(zs * 128, 128), 128)
         for f in range(4):
             out[f, :, lanes] = tile[f]
-        for f, (a, b) in enumerate(((0, 2), (1, 2), (3, 2), (0, 1))):
+        for f, (a, b) in enumerate(PRODUCTS):
             flux = tile[4 + f] - tile[a] * tile[b]
             out[4 + f, :, lanes] = flux
             if f < 3:
@@ -229,8 +236,8 @@
             out[8 + f, :, lanes] = -(wrecv[1, n, rows] - wrecv[0, n, rows]) * factor
 
     for n, k in enumerate(ORDER):
-        size = 256 if k else 224
-        pltpu.make_async_copy(send.at[n, pl.ds(0, size)], send.at[n, pl.ds(0, size)], send_sem.at[n]).wait()
+        sent = send.at[n, pl.ds(0, 8 if k else 7), pl.ds(0, SENT)]
+        pltpu.make_async_copy(sent, sent, send_sem.at[n]).wait()
         size = 64 if n else 56
         pltpu.make_async_copy(osend.at[n, pl.ds(0, size)], osend.at[n, pl.ds(0, size)], osend_sem.at[n]).wait()
         cross(n).wait_send()
@@ -258,13 +265,15 @@
             pltpu.SMEM((1,), F32),
             pltpu.VMEM((4, 32, GRID), F32),
             pltpu.VMEM((GRID, 128), F32),
-            pltpu.VMEM((4, 128, 256), F32),
+            pltpu.VMEM((4, 128, 192), F32),
             pltpu.VMEM((GRID + 1536, 256), BF16),
-            pltpu.VMEM((2, 7, 128, 256), BF16),
+            pltpu.VMEM((2, 7, 128, 192), BF16),
             pltpu.VMEM((256, GRID), BF16),
             pltpu.VMEM((256, GRID), BF16),
-            pltpu.VMEM((4, 256, 128), F32),
-            pltpu.VMEM((4, 256, 128), F32),
+            pltpu.VMEM((256, 128), F32),
+            pltpu.VMEM((4, 8, 32, 128), F32),
+            pltpu.VMEM((4, 8, 32, 128), F32),
+            pltpu.VMEM((4, 8, 8, 128), F32),
             pltpu.VMEM((2, 4, 64, 128), F32),
             pltpu.VMEM((4, 64, 128), F32),
             pltpu.VMEM((4, 64, 128), F32),

time: 47.7 us -> 45 us (0.943)
  Pallas kernels: 44.2 us -> 41.6 us
    pallas_call x1, Pallas kernels: 44.2 us -> 41.6 us  [shards(): pl.pallas_call(kernel, out_shape=jax.ShapeDtypeStruct((11, 8, TARGET), F3...]
where the time goes in v2:
time: 45 us; the launch traced here: 44.8 us
  Pallas kernels  41.6 us (92%)
  between operations  1.93 us (4%)
  local copies, waits for them, and re-layouts  1.28 us (3%)
    pallas_call x1, Pallas kernels, shards(): pl.pallas_call(kernel, out_shape=jax.ShapeDtypeStruct((11, 8, TARGET), F3...  41.6 us
    broadcast_in_dim x2, local copies, waits for them, and re-layouts, shards(): return (out[None, :4], out[None, 4:8], out[None, 8:])  1.28 us

profile of v2, /device:TPU:1, one launch (start us, length us, event | category | flops | bytes accessed | tf_op | source)
XLA Modules:
  0.0 44.8 jit_solution(15005126252909471380)
XLA Ops:
  1.9 41.6 %shard_map.76 = f32[11,8,512]{2,1,0:T(8,128)S(1)} custom-call(f32[1,4,32,2048]{3,2,1,0:T(8,128)} %fields.1, f32[1]{0:T(128)S(6)} %copy.8.density_hbm, f32[1]{0:T(128)S(6)} %copy.9.thickness_hbm, f32[2048,128]{1,0:T(8,128)} %constant.4.clone.col_hbm, f32[2,4,128,192]{3,2,1,0:T(8,128)} %constant.5.clone.row_hbm), custom_call_target="tpu_custom_call" | custom-call | tf_op jit(solution)/shard_map/pallas_call | solution.py:258
  43.5 0.7 %slice_bitcast_fusion = (f32[1,4,8,512]{3,2,1,0:T(8,128)}, f32[1,4,8,512]{3,2,1,0:T(8,128)}) fusion(f32[11,8,512]{2,1,0:T(8,128)S(1)} %shard_map.76), kind=kLoop, calls=%fused_computation | loop fusion | bytes 262144 | tf_op jit(solution)/shard_map/broadcast_in_dim | solution.py:296
  44.2 0.6 %slice_bitcast_fusion.2 = f32[1,3,8,512]{3,2,1,0:T(8,128)} fusion(f32[11,8,512]{2,1,0:T(8,128)S(1)} %shard_map.76), kind=kLoop, calls=%fused_computation.2 | loop fusion | bytes 98304 | tf_op jit(solution)/shard_map/broadcast_in_dim | solution.py:296

commit v3 on v2

--- a/solution.py
+++ b/solution.py
@@ -47,13 +47,36 @@
 def kernel(
     fields, density_hbm, thickness_hbm, col_hbm, row_hbm, out,
     density, thickness, g_in, col_in, row_in, col, row, g_high, g_low, whole, send, recv, local, acc, part_in, osend, orecv, wsend, wrecv,
-    load_sem, send_sem, recv_sem, part_sem, osend_sem, orecv_sem, wsend_sem, wrecv_sem,
+    load_sem, send_sem, recv_sem, part_sem, osend_sem, orecv_sem, wsend_sem, wrecv_sem, level_sem,
 ):
     slab, lev = lax.axis_index("slab"), lax.axis_index("lev")
     core, chip = lax.rem(slab, 2), lax.div(slab, 2)
     z, y = lax.div(chip, 8), lax.rem(chip, 8)
     has_up, has_down = lev < 7, lev > 0
+    even = lax.rem(lev, 2) == 0
+    neighbours = has_up.astype(jnp.int32) + has_down.astype(jnp.int32)
     near = [jnp.where(z < 2, jnp.where(z == 0, a, b), jnp.where(z == 2, c, d)) for a, b, c, d in zip(*NEAREST)]
+
+    barrier = pltpu.get_barrier_semaphore()
+
+    for i in reversed(range(4)):
+        for step in AROUND[0 if i else 1 :]:
+            peer = near[i] * 8 + lax.rem(y + step, 8)
+            pl.semaphore_signal(barrier, inc=1, device_id={"slab": 2 * peer + core})
+    pl.semaphore_signal(barrier, inc=1, device_id={"slab": 2 * chip + 1 - core})
+
+    def greet_levels(semaphore):
+        @pl.when(has_up)
+        def _():
+            pl.semaphore_signal(semaphore, inc=1, device_id={"lev": lev + 1})
+
+        @pl.when(has_down)
+        def _():
+            pl.semaphore_signal(semaphore, inc=1, device_id={"lev": lev - 1})
+
+    @pl.when(even)
+    def _():
+        greet_levels(barrier)
 
     load = pltpu.make_async_copy(fields.at[0], g_in, load_sem.at[0])
     load.start()
@@ -67,22 +90,6 @@
     ]
     for c in scalars:
         c.start()
-
-    barrier = pltpu.get_barrier_semaphore()
-
-    for i in reversed(range(4)):
-        for step in AROUND[0 if i else 1 :]:
-            peer = near[i] * 8 + lax.rem(y + step, 8)
-            pl.semaphore_signal(barrier, inc=1, device_id={"slab": 2 * peer + core})
-    pl.semaphore_signal(barrier, inc=1, device_id={"slab": 2 * chip + 1 - core})
-
-    @pl.when(has_up)
-    def _():
-        pl.semaphore_signal(barrier, inc=1, device_id={"lev": lev + 1})
-
-    @pl.when(has_down)
-    def _():
-        pl.semaphore_signal(barrier, inc=1, device_id={"lev": lev - 1})
 
     load.wait()
     fine = [g_in[f] for f in range(4)]
@@ -111,7 +118,12 @@
             send[n, f, 24:25] = jnp.sum(kept * alternating, axis=0, keepdims=True)
             local[zq, f] = 0.25 * kept
         if n == 0:
-            pl.semaphore_wait(barrier, 32 + has_up.astype(jnp.int32) + has_down.astype(jnp.int32))
+            pl.semaphore_wait(barrier, 32 + jnp.where(even, 0, neighbours))
+
+            @pl.when(jnp.logical_not(even))
+            def _():
+                greet_levels(level_sem)
+
 
         for step in AROUND[0 if k else 1 :]:
             yq = lax.rem(y + step, 8)
@@ -188,6 +200,10 @@
             device_id={"lev": lev + 1 if side == 0 else lev - 1},
         )
 
+    @pl.when(even)
+    def _():
+        pl.semaphore_wait(level_sem, neighbours)
+
     for n in range(4):
         zs = near[n]
         size = 64 if n else 56
@@ -218,23 +234,6 @@
     def _():
         wrecv[1] = jnp.zeros_like(wrecv[1])
 
-    factor = thickness[0] / (2.0 * density[0])
-    for n in range(4):
-        zs = near[n]
-        lanes = pl.ds(pl.multiple_of(zs * 128, 128), 128)
-
-        @pl.when(has_down)
-        def _(n=n):
-            lev_copy(n, 0).wait_recv()
-
-        @pl.when(has_up)
-        def _(n=n):
-            lev_copy(n, 1).wait_recv()
-
-        for f in range(3):
-            rows = slice(8 * f, 8 * f + 8)
-            out[8 + f, :, lanes] = -(wrecv[1, n, rows] - wrecv[0, n, rows]) * factor
-
     for n, k in enumerate(ORDER):
         sent = send.at[n, pl.ds(0, 8 if k else 7), pl.ds(0, SENT)]
         pltpu.make_async_copy(sent, sent, send_sem.at[n]).wait()
@@ -242,13 +241,24 @@
         pltpu.make_async_copy(osend.at[n, pl.ds(0, size)], osend.at[n, pl.ds(0, size)], osend_sem.at[n]).wait()
         cross(n).wait_send()
 
-        @pl.when(has_up)
-        def _(n=n):
+    @pl.when(has_down)
+    def _():
+        for n in range(4):
+            lev_copy(n, 1).wait_send()
+            lev_copy(n, 0).wait_recv()
+
+    @pl.when(has_up)
+    def _():
+        for n in range(4):
             lev_copy(n, 0).wait_send()
-
-        @pl.when(has_down)
-        def _(n=n):
-            lev_copy(n, 1).wait_send()
+            lev_copy(n, 1).wait_recv()
+
+    factor = thickness[0] / (2.0 * density[0])
+    for n in range(4):
+        lanes = pl.ds(pl.multiple_of(near[n] * 128, 128), 128)
+        for f in range(3):
+            rows = slice(8 * f, 8 * f + 8)
+            out[8 + f, :, lanes] = -(wrecv[1, n, rows] - wrecv[0, n, rows]) * factor
 
 
 def shards(columns, rows, fields, density, thickness):
@@ -288,6 +298,7 @@
             dma((4,)),
             dma((2, 4)),
             dma((2, 4)),
+            pltpu.SemaphoreType.REGULAR,
         ],
         compiler_params=pltpu.CompilerParams(
             collective_id=0, has_side_effects=True, vmem_limit_bytes=54528 * 1024

time: 45 us -> 44.2 us (0.982)
  Pallas kernels: 41.6 us -> 40.8 us
    pallas_call x1, Pallas kernels: 41.6 us -> 40.8 us  [shards(): pl.pallas_call(kernel, out_shape=jax.ShapeDtypeStruct((11, 8, TARGET), F3...]
where the time goes in v3:
time: 44.2 us; the launch traced here: 44 us
  Pallas kernels  40.8 us (92%)
  between operations  1.93 us (4%)
  local copies, waits for them, and re-layouts  1.28 us (3%)
    pallas_call x1, Pallas kernels, shards(): pl.pallas_call(kernel, out_shape=jax.ShapeDtypeStruct((11, 8, TARGET), F3...  40.8 us
    broadcast_in_dim x2, local copies, waits for them, and re-layouts, shards(): return (out[None, :4], out[None, 4:8], out[None, 8:])  1.28 us

profile of v3, /device:TPU:1, one launch (start us, length us, event | category | flops | bytes accessed | tf_op | source)
XLA Modules:
  0.0 44.0 jit_solution(3601514616015253691)
XLA Ops:
  1.9 40.8 %shard_map.76 = f32[11,8,512]{2,1,0:T(8,128)S(1)} custom-call(f32[1,4,32,2048]{3,2,1,0:T(8,128)} %fields.1, f32[1]{0:T(128)S(6)} %copy.8.density_hbm, f32[1]{0:T(128)S(6)} %copy.9.thickness_hbm, f32[2048,128]{1,0:T(8,128)} %constant.4.clone.col_hbm, f32[2,4,128,192]{3,2,1,0:T(8,128)} %constant.5.clone.row_hbm), custom_call_target="tpu_custom_call" | custom-call | tf_op jit(solution)/shard_map/pallas_call | solution.py:268
  42.7 0.7 %slice_bitcast_fusion = (f32[1,4,8,512]{3,2,1,0:T(8,128)}, f32[1,4,8,512]{3,2,1,0:T(8,128)}) fusion(f32[11,8,512]{2,1,0:T(8,128)S(1)} %shard_map.76), kind=kLoop, calls=%fused_computation | loop fusion | bytes 262144 | tf_op jit(solution)/shard_map/broadcast_in_dim | solution.py:307
  43.4 0.6 %slice_bitcast_fusion.2 = f32[1,3,8,512]{3,2,1,0:T(8,128)} fusion(f32[11,8,512]{2,1,0:T(8,128)S(1)} %shard_map.76), kind=kLoop, calls=%fused_computation.2 | loop fusion | bytes 98304 | tf_op jit(solution)/shard_map/broadcast_in_dim | solution.py:307

commit v4 on v3

--- a/solution.py
+++ b/solution.py
@@ -172,10 +172,10 @@
             else:
                 acc[half] = total
             if n == 3 and half == 0:
-                for i in reversed(range(4)):
+                for i in (1, 0, 2, 3):
                     cross(i).start()
 
-    for i in reversed(range(4)):
+    for i in (1, 0, 2, 3):
         zq = near[i]
         cross(i).wait_recv()
         osend[i] = acc[1, zq] + part_in[i]

time: 44.2 us -> 43.7 us (0.989)
  Pallas kernels: 40.8 us -> 40.3 us
    pallas_call x1, Pallas kernels: 40.8 us -> 40.3 us  [shards(): pl.pallas_call(kernel, out_shape=jax.ShapeDtypeStruct((11, 8, TARGET), F3...]
where the time goes in v4:
time: 43.7 us; the launch traced here: 43.5 us
  Pallas kernels  40.3 us (92%)
  between operations  1.93 us (4%)
  local copies, waits for them, and re-layouts  1.28 us (3%)
    pallas_call x1, Pallas kernels, shards(): pl.pallas_call(kernel, out_shape=jax.ShapeDtypeStruct((11, 8, TARGET), F3...  40.3 us
    broadcast_in_dim x2, local copies, waits for them, and re-layouts, shards(): return (out[None, :4], out[None, 4:8], out[None, 8:])  1.28 us

profile of v4, /device:TPU:1, one launch (start us, length us, event | category | flops | bytes accessed | tf_op | source)
XLA Modules:
  0.0 43.5 jit_solution(9880696132047792804)
XLA Ops:
  1.9 40.3 %shard_map.76 = f32[11,8,512]{2,1,0:T(8,128)S(1)} custom-call(f32[1,4,32,2048]{3,2,1,0:T(8,128)} %fields.1, f32[1]{0:T(128)S(6)} %copy.8.density_hbm, f32[1]{0:T(128)S(6)} %copy.9.thickness_hbm, f32[2048,128]{1,0:T(8,128)} %constant.4.clone.col_hbm, f32[2,4,128,192]{3,2,1,0:T(8,128)} %constant.5.clone.row_hbm), custom_call_target="tpu_custom_call" | custom-call | tf_op jit(solution)/shard_map/pallas_call | solution.py:268
  42.2 0.7 %slice_bitcast_fusion = (f32[1,4,8,512]{3,2,1,0:T(8,128)}, f32[1,4,8,512]{3,2,1,0:T(8,128)}) fusion(f32[11,8,512]{2,1,0:T(8,128)S(1)} %shard_map.76), kind=kLoop, calls=%fused_computation | loop fusion | bytes 262144 | tf_op jit(solution)/shard_map/broadcast_in_dim | solution.py:307
  42.9 0.6 %slice_bitcast_fusion.2 = f32[1,3,8,512]{3,2,1,0:T(8,128)} fusion(f32[11,8,512]{2,1,0:T(8,128)S(1)} %shard_map.76), kind=kLoop, calls=%fused_computation.2 | loop fusion | bytes 98304 | tf_op jit(solution)/shard_map/broadcast_in_dim | solution.py:307

commit v5 on v4

--- a/solution.py
+++ b/solution.py
@@ -12,6 +12,7 @@
 GRID = 2048
 TARGET = 512
 SENT = 25
+RELAYED = (0, 1)
 ORDER = (2, 1, 3, 0)
 PRODUCTS = ((0, 2), (1, 2), (3, 2), (0, 1))
 AROUND = (0, 4, 1, 5, 2, 6, 3, 7)
@@ -47,13 +48,13 @@
 def kernel(
     fields, density_hbm, thickness_hbm, col_hbm, row_hbm, out,
     density, thickness, g_in, col_in, row_in, col, row, g_high, g_low, whole, send, recv, local, acc, part_in, osend, orecv, wsend, wrecv,
-    load_sem, send_sem, recv_sem, part_sem, osend_sem, orecv_sem, wsend_sem, wrecv_sem, level_sem,
+    load_sem, send_sem, recv_sem, part_sem, osend_sem, orecv_sem, wsend_sem, wrecv_sem, relay_sem, level_sem,
 ):
     slab, lev = lax.axis_index("slab"), lax.axis_index("lev")
     core, chip = lax.rem(slab, 2), lax.div(slab, 2)
     z, y = lax.div(chip, 8), lax.rem(chip, 8)
     has_up, has_down = lev < 7, lev > 0
-    even = lax.rem(lev, 2) == 0
+    even, odd = lax.rem(lev, 2) == 0, lax.rem(lev, 2) == 1
     neighbours = has_up.astype(jnp.int32) + has_down.astype(jnp.int32)
     near = [jnp.where(z < 2, jnp.where(z == 0, a, b), jnp.where(z == 2, c, d)) for a, b, c, d in zip(*NEAREST)]
 
@@ -218,13 +219,33 @@
             if f < 3:
                 wsend[n, 8 * f : 8 * f + 8] = density[0] * flux
 
-        @pl.when(has_up)
+        @pl.when(even if n in RELAYED else has_up)
         def _(n=n):
             lev_copy(n, 0).start()
 
-        @pl.when(has_down)
+        @pl.when(odd if n in RELAYED else has_down)
         def _(n=n):
             lev_copy(n, 1).start()
+
+    def relay(n, side):
+        return pltpu.make_async_remote_copy(
+            src_ref=wrecv.at[1 - side, n],
+            dst_ref=wrecv.at[side, n],
+            send_sem=relay_sem.at[n],
+            recv_sem=wrecv_sem.at[side, n],
+            device_id={"lev": lev + 2 if side == 0 else lev - 2},
+        )
+
+    for mine, side, has_next in ((even, 0, lev < 6), (odd, 1, lev > 1)):
+
+        @pl.when(mine)
+        def _(side=side, has_next=has_next):
+            for n in RELAYED:
+                lev_copy(n, 1 - side).wait_recv()
+
+                @pl.when(has_next)
+                def _(n=n):
+                    relay(n, side).start()
 
     @pl.when(jnp.logical_not(has_down))
     def _():
@@ -241,17 +262,26 @@
         pltpu.make_async_copy(osend.at[n, pl.ds(0, size)], osend.at[n, pl.ds(0, size)], osend_sem.at[n]).wait()
         cross(n).wait_send()
 
-    @pl.when(has_down)
-    def _():
-        for n in range(4):
-            lev_copy(n, 1).wait_send()
-            lev_copy(n, 0).wait_recv()
-
-    @pl.when(has_up)
-    def _():
-        for n in range(4):
-            lev_copy(n, 0).wait_send()
-            lev_copy(n, 1).wait_recv()
+    for mine, side, has_next, has_other in ((even, 0, lev < 6, has_down), (odd, 1, lev > 1, has_up)):
+
+        @pl.when(mine)
+        def _(side=side, has_next=has_next, has_other=has_other):
+            for n in range(4):
+                lev_copy(n, side).wait_send()
+                if n not in RELAYED:
+                    lev_copy(n, 1 - side).wait_recv()
+
+            @pl.when(has_other)
+            def _():
+                for n in range(4):
+                    if n not in RELAYED:
+                        lev_copy(n, 1 - side).wait_send()
+                    lev_copy(n, side).wait_recv()
+
+            @pl.when(has_next)
+            def _():
+                for n in RELAYED:
+                    relay(n, side).wait_send()
 
     factor = thickness[0] / (2.0 * density[0])
     for n in range(4):
@@ -298,6 +328,7 @@
             dma((4,)),
             dma((2, 4)),
             dma((2, 4)),
+            dma((4,)),
             pltpu.SemaphoreType.REGULAR,
         ],
         compiler_params=pltpu.CompilerParams(

time: 43.7 us -> 43.6 us (level)
  no operation moved by 1% of the time
where the time goes in v5:
time: 43.6 us; the launch traced here: 43.4 us
  Pallas kernels  40.2 us (92%)
  between operations  1.93 us (4%)
  local copies, waits for them, and re-layouts  1.28 us (3%)
    pallas_call x1, Pallas kernels, shards(): pl.pallas_call(kernel, out_shape=jax.ShapeDtypeStruct((11, 8, TARGET), F3...  40.2 us
    broadcast_in_dim x2, local copies, waits for them, and re-layouts, shards(): return (out[None, :4], out[None, 4:8], out[None, 8:])  1.28 us

profile of v5, /device:TPU:1, one launch (start us, length us, event | category | flops | bytes accessed | tf_op | source)
XLA Modules:
  0.0 43.4 jit_solution(4755580328153601273)
XLA Ops:
  1.9 40.2 %shard_map.76 = f32[11,8,512]{2,1,0:T(8,128)S(1)} custom-call(f32[1,4,32,2048]{3,2,1,0:T(8,128)} %fields.1, f32[1]{0:T(128)S(6)} %copy.8.density_hbm, f32[1]{0:T(128)S(6)} %copy.9.thickness_hbm, f32[2048,128]{1,0:T(8,128)} %constant.4.clone.col_hbm, f32[2,4,128,192]{3,2,1,0:T(8,128)} %constant.5.clone.row_hbm), custom_call_target="tpu_custom_call" | custom-call | tf_op jit(solution)/shard_map/pallas_call | solution.py:298
  42.2 0.7 %slice_bitcast_fusion = (f32[1,4,8,512]{3,2,1,0:T(8,128)}, f32[1,4,8,512]{3,2,1,0:T(8,128)}) fusion(f32[11,8,512]{2,1,0:T(8,128)S(1)} %shard_map.76), kind=kLoop, calls=%fused_computation | loop fusion | bytes 262144 | tf_op jit(solution)/shard_map/broadcast_in_dim | solution.py:338
  42.8 0.6 %slice_bitcast_fusion.2 = f32[1,3,8,512]{3,2,1,0:T(8,128)} fusion(f32[11,8,512]{2,1,0:T(8,128)S(1)} %shard_map.76), kind=kLoop, calls=%fused_computation.2 | loop fusion | bytes 98304 | tf_op jit(solution)/shard_map/broadcast_in_dim | solution.py:338

commit v6 on v5

--- a/solution.py
+++ b/solution.py
@@ -27,7 +27,7 @@
     profile = (1.0 + 2.0 * np.cos(2.0 * np.pi * np.outer(offsets, k) / GRID).sum(1)) / GRID
     index = (GRID // TARGET * np.arange(TARGET)[:, None] - np.arange(GRID)[None, :]) % GRID
     matrix = profile[index].astype(np.float32)
-    columns = np.ascontiguousarray(matrix[:128].T)
+    columns = np.ascontiguousarray(matrix[:, :512].T)
     first = matrix[:, :512].reshape(4, 8, 2, 8, 8, 2, 8, 4)[..., 1:].swapaxes(6, 7)
     rows = [
         np.stack([first[:, :, c, :, :, core] for c in (1 - core, core)], axis=1).reshape(4, 128, 192)
@@ -58,6 +58,10 @@
     neighbours = has_up.astype(jnp.int32) + has_down.astype(jnp.int32)
     near = [jnp.where(z < 2, jnp.where(z == 0, a, b), jnp.where(z == 2, c, d)) for a, b, c, d in zip(*NEAREST)]
 
+    loads = [pltpu.make_async_copy(fields.at[0, f], g_in.at[f], load_sem.at[f]) for f in range(4)]
+    loads.append(pltpu.make_async_copy(col_hbm.at[pl.ds(0, 8)], col_in, load_sem.at[4]))
+    for c in reversed(loads):
+        c.start()
     barrier = pltpu.get_barrier_semaphore()
 
     for i in reversed(range(4)):
@@ -79,20 +83,24 @@
     def _():
         greet_levels(barrier)
 
-    load = pltpu.make_async_copy(fields.at[0], g_in, load_sem.at[0])
-    load.start()
-    col_load = pltpu.make_async_copy(col_hbm, col_in, load_sem.at[1])
-    col_load.start()
-    row_load = pltpu.make_async_copy(row_hbm.at[core], row_in, load_sem.at[2])
-    row_load.start()
-    scalars = [
-        pltpu.make_async_copy(density_hbm, density, load_sem.at[3]),
-        pltpu.make_async_copy(thickness_hbm, thickness, load_sem.at[4]),
-    ]
-    for c in scalars:
-        c.start()
-
-    load.wait()
+    loads[4].wait()
+    lane = lax.broadcasted_iota(jnp.int32, (8, 128), 1)
+    for shift in range(0, 128, 4):
+        for q in range(4):
+            pair = []
+            for turn in (shift, shift + 2):
+                here = col_in[:, 128 * q : 128 * q + 128]
+                if turn:
+                    before = col_in[:, 128 * ((q + 3) % 4) : 128 * ((q + 3) % 4) + 128]
+                    here = jnp.where(lane < turn, pltpu.roll(before, turn, 1), pltpu.roll(here, turn, 1))
+                pair.append(here)
+            h, l = split(jnp.concatenate(pair))
+            at = 512 * ((4 - q) % 4) + 4 * shift
+            col[at : at + 16, :128], col[at : at + 16, 128:] = h, l
+            if at < 1536:
+                col[GRID + at : GRID + at + 16, :128], col[GRID + at : GRID + at + 16, 128:] = h, l
+    for c in loads[:4]:
+        c.wait()
     fine = [g_in[f] for f in range(4)]
     fine += [fine[a] * fine[b] for a, b in PRODUCTS]
     for f in range(8):
@@ -100,10 +108,14 @@
         g_high[32 * f : 32 * f + 32] = h
         g_low[32 * f : 32 * f + 32] = l
 
-    col_load.wait()
-    h, l = split(col_in[...])
-    col[:GRID, :128], col[:GRID, 128:] = h, l
-    col[GRID:, :128], col[GRID:, 128:] = h[:1536], l[:1536]
+    row_load = pltpu.make_async_copy(row_hbm.at[core], row_in, load_sem.at[8])
+    row_load.start()
+    scalars = [
+        pltpu.make_async_copy(density_hbm, density, load_sem.at[9]),
+        pltpu.make_async_copy(thickness_hbm, thickness, load_sem.at[10]),
+    ]
+    for c in scalars:
+        c.start()
 
     alternating = 1.0 - 2.0 * lax.rem(lax.broadcasted_iota(jnp.int32, (8, 128), 0), 2).astype(F32)
     for n, k in enumerate(ORDER):
@@ -118,14 +130,15 @@
             kept = whole[pl.ds(32 * f, 8, 4)]
             send[n, f, 24:25] = jnp.sum(kept * alternating, axis=0, keepdims=True)
             local[zq, f] = 0.25 * kept
-        if n == 0:
-            pl.semaphore_wait(barrier, 32 + jnp.where(even, 0, neighbours))
-
-            @pl.when(jnp.logical_not(even))
-            def _():
-                greet_levels(level_sem)
-
-
+
+    pl.semaphore_wait(barrier, 32 + jnp.where(even, 0, neighbours))
+
+    @pl.when(jnp.logical_not(even))
+    def _():
+        greet_levels(level_sem)
+
+    for n, k in enumerate(ORDER):
+        zq = lax.rem(z + k, 4)
         for step in AROUND[0 if k else 1 :]:
             yq = lax.rem(y + step, 8)
             pltpu.make_async_remote_copy(
@@ -304,7 +317,7 @@
             pltpu.SMEM((1,), F32),
             pltpu.SMEM((1,), F32),
             pltpu.VMEM((4, 32, GRID), F32),
-            pltpu.VMEM((GRID, 128), F32),
+            pltpu.VMEM((8, 512), F32),
             pltpu.VMEM((4, 128, 192), F32),
             pltpu.VMEM((GRID + 1536, 256), BF16),
             pltpu.VMEM((2, 7, 128, 192), BF16),
@@ -320,7 +333,7 @@
             pltpu.VMEM((4, 64, 128), F32),
             pltpu.VMEM((4, 24, 128), F32),
             pltpu.VMEM((2, 4, 24, 128), F32),
-            dma((5,)),
+            dma((11,)),
             dma((4,)),
             dma((4,)),
             dma((2, 4)),

time: 43.6 us -> 44 us (level)
  no operation moved by 1% of the time
where the time goes in v6:
time: 44 us; the launch traced here: 43.6 us
  Pallas kernels  40.4 us (92%)
  between operations  1.93 us (4%)
  local copies, waits for them, and re-layouts  1.28 us (3%)
    pallas_call x1, Pallas kernels, shards(): pl.pallas_call(kernel, out_shape=jax.ShapeDtypeStruct((11, 8, TARGET), F3...  40.4 us
    broadcast_in_dim x2, local copies, waits for them, and re-layouts, shards(): return (out[None, :4], out[None, 4:8], out[None, 8:])  1.28 us

profile of v6, /device:TPU:1, one launch (start us, length us, event | category | flops | bytes accessed | tf_op | source)
XLA Modules:
  0.0 43.6 jit_solution(15647284377918750067)
XLA Ops:
  1.9 40.4 %shard_map.76 = f32[11,8,512]{2,1,0:T(8,128)S(1)} custom-call(f32[1,4,32,2048]{3,2,1,0:T(8,128)} %fields.1, f32[1]{0:T(128)S(6)} %copy.8.density_hbm, f32[1]{0:T(128)S(6)} %copy.9.thickness_hbm, f32[512,512]{1,0:T(8,128)} %constant.4.clone.col_hbm, f32[2,4,128,192]{3,2,1,0:T(8,128)} %constant.5.clone.row_hbm), custom_call_target="tpu_custom_call" | custom-call | tf_op jit(solution)/shard_map/pallas_call | solution.py:311
  42.3 0.7 %slice_bitcast_fusion = (f32[1,4,8,512]{3,2,1,0:T(8,128)}, f32[1,4,8,512]{3,2,1,0:T(8,128)}) fusion(f32[11,8,512]{2,1,0:T(8,128)S(1)} %shard_map.76), kind=kLoop, calls=%fused_computation | loop fusion | bytes 262144 | tf_op jit(solution)/shard_map/broadcast_in_dim | solution.py:351
  43.0 0.6 %slice_bitcast_fusion.2 = f32[1,3,8,512]{3,2,1,0:T(8,128)} fusion(f32[11,8,512]{2,1,0:T(8,128)S(1)} %shard_map.76), kind=kLoop, calls=%fused_computation.2 | loop fusion | bytes 98304 | tf_op jit(solution)/shard_map/broadcast_in_dim | solution.py:351
